TPU v7x, 128 devices: a whole 4x4x4 slice. The times are simulated.
128 devices in a mesh: wide: 8 (over y, core), grp: 16 (over z, x).
Axes of the slice: x: 4, y: 4, z: 4, core: 2. Of those that a mesh axis runs over, the one named last changes fastest.
Arguments:
- integrals: float32 [1200, 64, 1200], P('grp', 'wide'), may hold values from -6 to 6
- coeffs: float32 [1200, 800], replicated, may hold values from -0.1875 to 0.1875
Outputs:
- slab: float32 [800, 800, 64], P('grp', 'wide')
All inputs are finite; a program needn't handle non-finite values.
Results may differ from a plain program's by a relative error of at most 0.00007.
Values sent between devices are 32-bit elements; how exact they have to be, the bound alone decides.
A program may use at most 128 MiB of HBM per device.

v0:
```python
import jax
import jax.numpy as jnp
from jax import lax
from jax.sharding import PartitionSpec as P


def on_device(integrals, coeffs):
    cols, pair_dev, nao = integrals.shape
    offset = lax.axis_index("grp") * cols
    row_index = offset + jnp.arange(cols, dtype=jnp.int32)
    basis = jnp.arange(nao, dtype=jnp.int32)
    lower_mask = basis[None, :] <= row_index[:, None]
    received = lax.all_to_all(integrals, "grp", split_axis=2, concat_axis=0, tiled=True)
    mirrored = jnp.transpose(received, (2, 1, 0))
    symmetric = jnp.where(lower_mask[:, None, :], integrals, mirrored)
    half_done = jnp.einsum("spt,tk->spk", symmetric, coeffs, precision=lax.Precision.HIGHEST)
    own_coeffs = lax.dynamic_slice_in_dim(coeffs, offset, cols, 0)
    slab_local = lax.psum_scatter(
        jnp.einsum("spk,sl->klp", half_done, own_coeffs, precision=lax.Precision.HIGHEST),
        "grp",
        scatter_dimension=0,
        tiled=True,
    )
    return lax.all_to_all(slab_local, "wide", split_axis=1, concat_axis=2, tiled=True)


def solution(mesh):
    return jax.shard_map(
        on_device,
        mesh=mesh,
        in_specs=(P("grp", "wide", None), P()),
        out_specs=P("grp", "wide", None),
        check_vma=False,
    )
```

profile of v0, /device:TPU:1, one launch (start us, length us, event | category | flops | bytes accessed | tf_op | source)
XLA Modules:
  0.0 359.3 jit_solution(9798312822725288421)
XLA Ops:
  6.5 5.4 %copy.23 = f32[75,8,1200]{0,1,2:T(8,128)} copy(f32[75,8,1200]{2,1,0:T(8,128)} %param.2) | data formatting | bytes 5760000 | tf_op args[0]
  11.9 8.5 %all-to-all-start = ((f32[75,8,1200]{0,1,2:T(8,128)}), f32[75,8,1200]{0,1,2:T(8,128)}, u32[]{:S(2)}, u32[]{:S(2)}) async-start(f32[75,8,1200]{0,1,2:T(8,128)} %copy.23), calls=%async_computation | async-start | bytes 9830400 | tf_op jit(solution)/shard_map/all_to_all | solution.py:13
  20.4 0.0 reduce-scatter.4.cloned.1.call-start
  20.5 0.1 iota_compare_fusion
  20.6 72.5 %all-to-all-done = f32[75,8,1200]{0,1,2:T(8,128)} async-done(((f32[75,8,1200]{0,1,2:T(8,128)}), f32[75,8,1200]{0,1,2:T(8,128)}, u32[]{:S(2)}, u32[]{:S(2)}) %all-to-all-start) | async-done | bytes 2880032 | tf_op jit(solution)/shard_map/all_to_all | solution.py:13
  93.1 5.8 %copy.24 = f32[16,75,8,75]{1,0,2,3:T(8,128)} copy(f32[16,75,8,75]{1,2,3,0:T(8,128)} %bitcast.2) | data formatting | bytes 5760000 | tf_op jit(solution)/shard_map/all_to_all | solution.py:13
  98.8 0.0 copy-start
  98.8 5.8 %all_to_all.29 = f32[1200,8,75]{0,1,2:T(8,128)} reshape(f32[16,75,8,75]{1,0,2,3:T(8,128)} %copy.24) | data formatting | bytes 5760000 | tf_op jit(solution)/shard_map/all_to_all | solution.py:13
  104.6 0.0 copy-done
  104.6 0.0 copy-start.1
  104.6 2.5 bitcast_select_fusion
  107.1 0.6 copy-done.1
  107.7 11.2 %fusion = f32[75,8,800]{2,0,1:T(8,128)S(1)} fusion(f32[1200,800]{0,1:T(8,128)S(1)} %copy-done.1, f32[75,8,1200]{2,1,0:T(8,128)S(1)} %bitcast_select_fusion), kind=kOutput, calls=%fused_computation.1 | convolution fusion | flops 6912000000 | bytes 8640000 | tf_op jit(solution)/shard_map/spt,tk->spk/dot_general | solution.py:16
  118.9 21.3 %convolution_bitcast_fusion = f32[800,800,8]{0,1,2:T(8,128)} fusion(f32[75,8,800]{2,0,1:T(8,128)S(1)} %fusion, f32[1200,800]{0,1:T(8,128)S(1)} %copy-done.1, s32[]{:T(128)S(6)} %select_n.7), kind=kOutput, calls=%fused_computation | convolution fusion | flops 4608000000 | bytes 23183364 | tf_op jit(solution)/shard_map/spk,sl->klp/dot_general | solution.py:19
  140.2 24.0 %copy.26 = f32[800,800,8]{1,2,0:T(8,128)} copy(f32[800,800,8]{0,1,2:T(8,128)} %convolution_bitcast_fusion) | data formatting | bytes 40960000 | tf_op jit(solution)/shard_map/spk,sl->klp/transpose | solution.py:19
  164.2 0.0 reduce-scatter.4.cloned.1.call-update
  164.3 143.4 %reduce-scatter.4.cloned.1.call-done = f32[50,800,8]{1,2,0:T(8,128)} async-done(((f32[800,800,8]{1,2,0:T(8,128)}), f32[50,800,8]{1,2,0:T(8,128)}) %reduce-scatter.4.cloned.1.call-update) | async-done | bytes 1280016
  307.6 3.2 copy.27
  310.8 4.6 %reshape.24 = f32[8,1,40000]{2,1,0:T(1,128)} reshape(f32[800,8,50]{2,1,0:T(8,128)S(1)} %bitcast.27) | data formatting | bytes 2560000
  315.5 22.5 %all_to_all.36 = f32[8,1,40000]{2,1,0:T(1,128)S(1)} all-to-all(f32[8,1,40000]{2,1,0:T(1,128)} %reshape.24), channel_id=1, replica_groups=mesh['wide'=8,'grp'=16] {'wide'}, dimensions={0} | all-to-all | bytes 2560000 | tf_op jit(solution)/shard_map/all_to_all | solution.py:24
  338.0 0.5 broadcast.14
  338.6 5.1 %reduce = f32[8,40000]{1,0:T(8,128)} reduce(f32[8,1,40000]{2,1,0:T(1,128)S(1)} %all_to_all.36, f32[]{:T(128)} %broadcast.14), dimensions={1}, to_apply=%all_to_all.30.reduce_sub_computation | reduce | bytes 2560004 | tf_op jit(solution)/shard_map/all_to_all | solution.py:24
  343.7 5.9 %reshape.25 = f32[800,8,50]{2,1,0:T(8,128)S(1)} reshape(f32[8,40000]{1,0:T(8,128)} %reduce) | data formatting | bytes 2560000
  349.5 2.9 copy.29
  (1 shorter events, 0.0 us)
Async XLA Ops:
  11.9 81.2 %all-to-all-start = ((f32[75,8,1200]{0,1,2:T(8,128)}), f32[75,8,1200]{0,1,2:T(8,128)}, u32[]{:S(2)}, u32[]{:S(2)}) async-start(f32[75,8,1200]{0,1,2:T(8,128)} %copy.23), calls=%async_computation | async-start | bytes 9830400 | tf_op jit(solution)/shard_map/all_to_all | solution.py:13
  20.4 287.2 %reduce-scatter.4.cloned.1.call-start = ((), (), s32[]{:S(2)}) async-start(), calls=%async_computation.3 | async-start | bytes 24371200
  98.8 5.8 %copy-start = (f32[75,8,1200]{2,1,0:T(8,128)S(1)}, f32[75,8,1200]{2,1,0:T(8,128)}, u32[]{:S(2)}) copy-start(f32[75,8,1200]{2,1,0:T(8,128)} %param.2) | copy-start | bytes 8640004
  104.6 3.1 copy-start.1
Sparse Core Ops, SparseCore 0:
  164.4 143.1 reduce-scatter.3
where the time goes:
time: 360 us; the launch traced here: 359 us
  waiting for transfers between devices  216 us (60%)
  local copies, waits for them, and re-layouts  58.7 us (16%)
  matrix products  32.5 us (9%)
  blocking collectives  22.5 us (6%)
  between operations  13.5 us (4%)
  starting transfers between devices  8.51 us (2%)
  other arithmetic  7.69 us (2%)
    unnamed x2, waiting for transfers between devices  143 us
    all_to_all x1, waiting for transfers between devices, on_device(): lax.all_to_all(integrals, 'grp', split_axis=2, concat_axis=0, tiled=True)  72.5 us
    transpose x1, local copies, waits for them, and re-layouts, on_device(): jnp.einsum('spk,sl->klp', half_done, own_coeffs, precision=lax.Precision....  24 us
    all_to_all x1, blocking collectives, on_device(): lax.all_to_all(slab_local, 'wide', split_axis=1, concat_axis=2, tiled=True)  22.5 us
    dot_general x1, matrix products, on_device(): jnp.einsum('spk,sl->klp', half_done, own_coeffs, precision=lax.Precision....  21.3 us
    unnamed x7, local copies, waits for them, and re-layouts  16.5 us
    all_to_all x2, local copies, waits for them, and re-layouts, on_device(): lax.all_to_all(integrals, 'grp', split_axis=2, concat_axis=0, tiled=True)  11.5 us
    dot_general x1, matrix products, on_device(): jnp.einsum('spt,tk->spk', symmetric, coeffs, precision=lax.Precision.HIGH...  11.2 us
  transfers between devices with their start and end apart: 2, of which 2 were waited for; matrix products, arithmetic and copies ran while one was open for 0% of the time, Pallas kernels for 0%

commit v1 on v0

v1 whole, which is shorter than its diff:
```python
import functools

import jax
import jax.numpy as jnp
from jax import lax
from jax.experimental import pallas as pl
from jax.experimental.pallas import tpu as pltpu
from jax.sharding import PartitionSpec as P

MESH = pl.DeviceIdType.MESH
F32 = jnp.float32
BF16 = jnp.bfloat16
NT = (((1,), (1,)), ((), ()))
NN = (((1,), (0,)), ((), ()))

ROWS = 75
BAND = 80
OWN = 8
NAO = 1200
DEPTH = 1280
COLS = 100
KROWS = 50
SLOT = 56
PAIRS = 64


def split(v):
    hi = v.astype(BF16)
    return hi, (v - hi.astype(F32)).astype(BF16)


def widen(v):
    return jnp.concatenate([v, jnp.zeros((v.shape[0], DEPTH - NAO), F32)], axis=1)


def dot3(ah, al, bh, bl, dims):
    dot = functools.partial(lax.dot_general, dimension_numbers=dims, preferred_element_type=F32)
    return dot(ah, bh) + (dot(ah, bl) + dot(al, bh))


def kernel(x_ref, ct_ref, out_ref, xbuf, cbuf, th, tl, ch, cl, sent, got, ah, al, m, xr, n_, o,
           xsem, csem, s1, r1, l1, sx, rx, s2, r2, l2):
    g = lax.axis_index("grp")
    w = lax.axis_index("wide")
    y, c = w // 2, lax.rem(w, 2)
    other = 1 - c
    barrier = pltpu.get_barrier_semaphore()

    loads = [pltpu.make_async_copy(ct_ref, cbuf.at[pl.ds(0, 800), :], csem)]
    for p in range(OWN):
        loads.append(pltpu.make_async_copy(x_ref.at[:, p, :], xbuf.at[p], xsem.at[p]))
    for load in loads:
        load.start()

    src1 = g // 8
    src2 = y // 2

    def greet1(d, carry):
        gs = lax.rem(g + d, 16)

        @pl.when((d != 0) | (src1 != c))
        def _():
            pl.semaphore_signal(barrier, inc=1, device_id=(y * 2 + src1, gs), device_id_type=MESH)
        return carry

    lax.fori_loop(0, 16, greet1, 0)
    pl.semaphore_signal(barrier, inc=1, device_id=(y * 2 + other, g), device_id_type=MESH)

    def greet2(d, carry):
        gs = lax.rem(g + d // 4, 16)
        ws = lax.rem(y + lax.rem(d, 4), 4) * 2 + src2

        @pl.when((gs != g) | (ws != w))
        def _():
            pl.semaphore_signal(barrier, inc=1, device_id=(ws, gs), device_id_type=MESH)
        return carry

    lax.fori_loop(0, 64, greet2, 0)

    loads[0].wait()
    lane = lax.broadcasted_iota(jnp.int32, (16, DEPTH), 1)
    row = lax.broadcasted_iota(jnp.int32, (16, DEPTH), 0)
    for v in range(8):
        for b in range(7):
            value = widen(cbuf[pl.ds(COLS * v + 16 * b, 16), :])
            keep = lane < NAO
            if b == 6:
                keep = keep & (row < COLS - 96)
            hi, lo = split(jnp.where(keep, value, 0.0))
            ch[pl.ds(128 * v + 16 * b, 16), :] = hi
            cl[pl.ds(128 * v + 16 * b, 16), :] = lo
        ch[pl.ds(128 * v + 112, 16), :] = jnp.zeros((16, DEPTH), BF16)
        cl[pl.ds(128 * v + 112, 16), :] = jnp.zeros((16, DEPTH), BF16)

    for p in range(OWN):
        loads[1 + p].wait()
        for b in range(5):
            height = min(16, ROWS - 16 * b)
            value = widen(xbuf[p, pl.ds(16 * b, height), :])
            if height < 16:
                value = jnp.concatenate([value, jnp.zeros((16 - height, DEPTH), F32)], axis=0)
            local = row + 16 * b
            s = local + ROWS * g
            value = jnp.where(lane < s, value, jnp.where(lane == s, 0.5 * value, 0.0))
            if b == 4:
                value = jnp.where(local < ROWS, value, 0.0)
            hi, lo = split(value)
            th[pl.ds(BAND * p + 16 * b, 16), :] = hi
            tl[pl.ds(BAND * p + 16 * b, 16), :] = lo

    for n in range(4):
        got[n, pl.ds(NAO, DEPTH - NAO), :] = jnp.zeros((DEPTH - NAO, 128), F32)

    pl.semaphore_wait(barrier, 16 + 1 + 64 - jnp.where(src1 == c, 1, 0) - jnp.where(src2 == c, 1, 0))

    def stage1(q, carry):
        base = pl.multiple_of(q * 256, 256)
        bh = ch[pl.ds(base, 256), :]
        bl = cl[pl.ds(base, 256), :]
        acc = dot3(th[...], tl[...], bh, bl, NT)
        for e in range(2):
            sent[2 * q + e] = acc[:, 128 * e:128 * (e + 1)]
        c2 = q // 2
        wd = y * 2 + c2

        def send(k, carry):
            i = lax.rem(k // 2 + g, 8)
            e = lax.rem(k, 2)
            j = 8 * c + i
            tile = lax.rem(2 * q, 4) + e
            src = sent.at[2 * q + e, pl.ds(i * BAND, ROWS), :]
            dst = got.at[tile, pl.ds(ROWS * g, ROWS), :]

            @pl.when((j != g) | (c2 != c))
            def _():
                pltpu.make_async_remote_copy(
                    src_ref=src, dst_ref=dst, send_sem=s1.at[q, k], recv_sem=r1.at[tile, g],
                    device_id=(wd, j), device_id_type=MESH).start()

            @pl.when((j == g) & (c2 == c))
            def _():
                pltpu.make_async_copy(src, dst, l1.at[e]).start()
                pltpu.make_async_copy(src, dst, l1.at[e]).wait()
            return carry

        lax.fori_loop(0, 16, send, 0)
        return carry

    lax.fori_loop(0, 4, stage1, 0)

    for h in range(2):
        def arrive(k, carry):
            tile, gs = 2 * h + k // 16, lax.rem(k, 16)

            @pl.when((gs != g) | (src1 != c))
            def _():
                pltpu.make_async_remote_copy(
                    src_ref=sent.at[0, pl.ds(0, ROWS), :], dst_ref=got.at[tile, pl.ds(ROWS * gs, ROWS), :],
                    send_sem=s1.at[0, 0], recv_sem=r1.at[tile, gs], device_id=(w, g), device_id_type=MESH).wait_recv()
            return carry

        lax.fori_loop(0, 32, arrive, 0)

        def halves(b, carry):
            at = pl.multiple_of(b * 128, 128)
            for e in range(2):
                hi, lo = split(got[2 * h + e, pl.ds(at, 128), :])
                ah[pl.ds(at, 128), pl.ds(128 * e, 128)] = hi
                al[pl.ds(at, 128), pl.ds(128 * e, 128)] = lo
            return carry

        lax.fori_loop(0, DEPTH // 128, halves, 0)

        def rows_of(half, carry):
            at = pl.multiple_of(lax.rem(half + other, 2) * 512, 512)
            acc = dot3(ch[pl.ds(at, 512), :], cl[pl.ds(at, 512), :], ah[...], al[...], NN)
            for e in range(2):
                m[2 * h + e, pl.ds(at, 512), :] = acc[:, 128 * e:128 * (e + 1)]

            @pl.when(half == 0)
            def _():
                for e in range(2):
                    pltpu.make_async_remote_copy(
                        src_ref=m.at[2 * h + e, pl.ds(at, 512), :], dst_ref=xr.at[2 * h + e],
                        send_sem=sx.at[2 * h + e], recv_sem=rx.at[2 * h + e],
                        device_id=(y * 2 + other, g), device_id_type=MESH).start()
            return carry

        lax.fori_loop(0, 2, rows_of, 0)

    pair = 16 * y + g

    def spread(n, half, a):
        v = 4 * half + a
        wd = 4 * c + n
        for r in range(2):
            gd = 2 * v + r
            src = n_.at[n, pl.ds(v * 128 + r * KROWS, KROWS), :]
            dst = o.at[pl.ds(pair * SLOT, KROWS), :]

            @pl.when((gd != g) | (wd != w))
            def _():
                pltpu.make_async_remote_copy(
                    src_ref=src, dst_ref=dst, send_sem=s2.at[n, gd], recv_sem=r2.at[pair],
                    device_id=(wd, gd), device_id_type=MESH).start()

            @pl.when((gd == g) & (wd == w))
            def _():
                pltpu.make_async_copy(src, dst, l2).start()
                pltpu.make_async_copy(src, dst, l2).wait()

    def own(t, carry):
        n, a = t // 4, lax.rem(t, 4)
        at = pl.multiple_of((4 * c + a) * 128, 128)
        back = pl.multiple_of((4 * c + n) * 128, 128)
        n_[n, pl.ds(at, 128), :] = m[n, pl.ds(at, 128), :] + m[a, pl.ds(back, 128), :].T
        spread(n, c, a)
        return carry

    lax.fori_loop(0, 16, own, 0)

    for n in range(4):
        pltpu.make_async_remote_copy(
            src_ref=m.at[n, pl.ds(0, 512), :], dst_ref=xr.at[n], send_sem=sx.at[n], recv_sem=rx.at[n],
            device_id=(w, g), device_id_type=MESH).wait()

    def cross(t, carry):
        n, a = t // 4, lax.rem(t, 4)
        at = pl.multiple_of((4 * other + a) * 128, 128)
        n_[n, pl.ds(at, 128), :] = m[n, pl.ds(at, 128), :] + xr[a, pl.ds(pl.multiple_of(n * 128, 128), 128), :].T
        spread(n, other, a)
        return carry

    lax.fori_loop(0, 16, cross, 0)

    def left1(k, carry):
        q, kk = k // 16, lax.rem(k, 16)
        j = 8 * c + lax.rem(kk // 2 + g, 8)

        @pl.when((j != g) | (q // 2 != c))
        def _():
            pltpu.make_async_remote_copy(
                src_ref=sent.at[0, pl.ds(0, ROWS), :], dst_ref=got.at[0, pl.ds(0, ROWS), :],
                send_sem=s1.at[q, kk], recv_sem=r1.at[0, 0], device_id=(w, g), device_id_type=MESH).wait_send()
        return carry

    lax.fori_loop(0, 64, left1, 0)

    def left2(k, carry):
        n, gd = k // 16, lax.rem(k, 16)

        @pl.when((gd != g) | (4 * c + n != w))
        def _():
            pltpu.make_async_remote_copy(
                src_ref=n_.at[0, pl.ds(0, KROWS), :], dst_ref=o.at[pl.ds(0, KROWS), :],
                send_sem=s2.at[n, gd], recv_sem=r2.at[0], device_id=(w, g), device_id_type=MESH).wait_send()
        return carry

    lax.fori_loop(0, 64, left2, 0)

    def landed(q, carry):
        @pl.when((q != pair) | (src2 != c))
        def _():
            pltpu.make_async_remote_copy(
                src_ref=n_.at[0, pl.ds(0, KROWS), :], dst_ref=o.at[pl.ds(q * SLOT, KROWS), :],
                send_sem=s2.at[0, 0], recv_sem=r2.at[q], device_id=(w, g), device_id_type=MESH).wait_recv()
        return carry

    lax.fori_loop(0, PAIRS, landed, 0)

    def gather(k, carry):
        for b in range(PAIRS // 8):
            out_ref[k, pl.ds(8 * b, 8), :] = o[pl.ds(8 * b * SLOT + k, 8, stride=SLOT), :][:, :COLS]
        return carry

    lax.fori_loop(0, KROWS, gather, 0)


def on_device(integrals, coeffs):
    dma = pltpu.SemaphoreType.DMA
    slab = pl.pallas_call(
        kernel,
        out_shape=jax.ShapeDtypeStruct((KROWS, PAIRS, COLS), F32),
        in_specs=[pl.BlockSpec(memory_space=pl.ANY)] * 2,
        out_specs=pl.BlockSpec(memory_space=pltpu.VMEM),
        scratch_shapes=[
            pltpu.VMEM((OWN, ROWS, NAO), F32),
            pltpu.VMEM((816, NAO), F32),
            pltpu.VMEM((OWN * BAND, DEPTH), BF16),
            pltpu.VMEM((OWN * BAND, DEPTH), BF16),
            pltpu.VMEM((1024, DEPTH), BF16),
            pltpu.VMEM((1024, DEPTH), BF16),
            pltpu.VMEM((8, OWN * BAND, 128), F32),
            pltpu.VMEM((4, DEPTH, 128), F32),
            pltpu.VMEM((DEPTH, 256), BF16),
            pltpu.VMEM((DEPTH, 256), BF16),
            pltpu.VMEM((4, 1024, 128), F32),
            pltpu.VMEM((4, 512, 128), F32),
            pltpu.VMEM((4, 1024, 128), F32),
            pltpu.VMEM((PAIRS * SLOT, 128), F32),
            dma((OWN,)), dma,
            dma((4, 16)), dma((4, 16)), dma((2,)),
            dma((4,)), dma((4,)),
            dma((4, 16)), dma((PAIRS,)), dma,
        ],
        compiler_params=pltpu.CompilerParams(
            collective_id=0, has_side_effects=True, vmem_limit_bytes=60 * 2**20),
    )(integrals, coeffs.T)
    return jnp.transpose(slab, (0, 2, 1))


def solution(mesh):
    return jax.shard_map(
        on_device,
        mesh=mesh,
        in_specs=(P("grp", "wide", None), P()),
        out_specs=P("grp", "wide", None),
        check_vma=False,
    )
```

time: 360 us -> 88.4 us (0.25)
  the two profiles are of different devices: /device:TPU:1 before, /device:TPU:25 now
where the time goes in v1:
time: 88.4 us; the launch traced here: 88.3 us
  Pallas kernels  85.5 us (97%)
  local copies, waits for them, and re-layouts  2.78 us (3%)
    pallas_call x1, Pallas kernels, on_device(): pl.pallas_call(kernel, out_shape=jax.ShapeDtypeStruct((KROWS, PAIRS, COLS...  85.5 us
    unnamed x1, local copies, waits for them, and re-layouts  2.78 us

profile of v1, /device:TPU:25, one launch (start us, length us, event | category | flops | bytes accessed | tf_op | source)
XLA Modules:
  0.0 88.3 jit_solution(11945396855161251302)
XLA Ops:
  0.0 85.5 %shard_map.28 = f32[50,64,100]{2,1,0:T(8,128)} custom-call(f32[75,8,1200]{2,1,0:T(8,128)} %x_ref.1, f32[800,1200]{1,0:T(8,128)} %bitcast.3), custom_call_target="tpu_custom_call" | custom-call | tf_op jit(solution)/shard_map/pallas_call | solution.py:281
  85.5 2.8 %copy.4 = f32[50,100,64]{1,2,0:T(8,128)} copy(f32[50,100,64]{1,2,0:T(8,128)} %bitcast.2) | data formatting | bytes 2560000

commit v2 on v1

--- a/solution.py
+++ b/solution.py
@@ -39,7 +39,7 @@
 
 
 def kernel(x_ref, ct_ref, out_ref, xbuf, cbuf, th, tl, ch, cl, sent, got, ah, al, m, xr, n_, o,
-           xsem, csem, s1, r1, l1, sx, rx, s2, r2, l2):
+           xsem, csem, s1, r1, l1, sx, rx, s2, r2, l2, ready):
     g = lax.axis_index("grp")
     w = lax.axis_index("wide")
     y, c = w // 2, lax.rem(w, 2)
@@ -64,18 +64,13 @@
         return carry
 
     lax.fori_loop(0, 16, greet1, 0)
-    pl.semaphore_signal(barrier, inc=1, device_id=(y * 2 + other, g), device_id_type=MESH)
-
     def greet2(d, carry):
-        gs = lax.rem(g + d // 4, 16)
-        ws = lax.rem(y + lax.rem(d, 4), 4) * 2 + src2
-
-        @pl.when((gs != g) | (ws != w))
-        def _():
-            pl.semaphore_signal(barrier, inc=1, device_id=(ws, gs), device_id_type=MESH)
-        return carry
-
-    lax.fori_loop(0, 64, greet2, 0)
+        @pl.when(d != w)
+        def _():
+            pl.semaphore_signal(barrier, inc=1, device_id=(d, g), device_id_type=MESH)
+        return carry
+
+    lax.fori_loop(0, 8, greet2, 0)
 
     loads[0].wait()
     lane = lax.broadcasted_iota(jnp.int32, (16, DEPTH), 1)
@@ -111,23 +106,31 @@
     for n in range(4):
         got[n, pl.ds(NAO, DEPTH - NAO), :] = jnp.zeros((DEPTH - NAO, 128), F32)
 
-    pl.semaphore_wait(barrier, 16 + 1 + 64 - jnp.where(src1 == c, 1, 0) - jnp.where(src2 == c, 1, 0))
+    pl.semaphore_wait(barrier, 16 + 7 - jnp.where(src1 == c, 1, 0))
+
+    def pass_on(d, carry):
+        @pl.when(d != w)
+        def _():
+            pl.semaphore_signal(ready, inc=1, device_id=(d, g), device_id_type=MESH)
+        return carry
+
+    lax.fori_loop(0, 8, pass_on, 0)
 
     def stage1(q, carry):
-        base = pl.multiple_of(q * 256, 256)
+        c2, h = lax.rem(q, 2), q // 2
+        base = pl.multiple_of(c2 * 512 + h * 256, 256)
         bh = ch[pl.ds(base, 256), :]
         bl = cl[pl.ds(base, 256), :]
         acc = dot3(th[...], tl[...], bh, bl, NT)
         for e in range(2):
             sent[2 * q + e] = acc[:, 128 * e:128 * (e + 1)]
-        c2 = q // 2
         wd = y * 2 + c2
 
         def send(k, carry):
             i = lax.rem(k // 2 + g, 8)
             e = lax.rem(k, 2)
             j = 8 * c + i
-            tile = lax.rem(2 * q, 4) + e
+            tile = 2 * h + e
             src = sent.at[2 * q + e, pl.ds(i * BAND, ROWS), :]
             dst = got.at[tile, pl.ds(ROWS * g, ROWS), :]
 
@@ -148,8 +151,10 @@
 
     lax.fori_loop(0, 4, stage1, 0)
 
-    for h in range(2):
-        def arrive(k, carry):
+    pair = 16 * y + g
+
+    def arrive(h):
+        def one(k, carry):
             tile, gs = 2 * h + k // 16, lax.rem(k, 16)
 
             @pl.when((gs != g) | (src1 != c))
@@ -159,8 +164,9 @@
                     send_sem=s1.at[0, 0], recv_sem=r1.at[tile, gs], device_id=(w, g), device_id_type=MESH).wait_recv()
             return carry
 
-        lax.fori_loop(0, 32, arrive, 0)
-
+        lax.fori_loop(0, 32, one, 0)
+
+    def multiply(h):
         def halves(b, carry):
             at = pl.multiple_of(b * 128, 128)
             for e in range(2):
@@ -188,56 +194,71 @@
 
         lax.fori_loop(0, 2, rows_of, 0)
 
-    pair = 16 * y + g
-
-    def spread(n, half, a):
+    def crossed(h):
+        for n in (2 * h, 2 * h + 1):
+            pltpu.make_async_remote_copy(
+                src_ref=m.at[n, pl.ds(0, 512), :], dst_ref=xr.at[n], send_sem=sx.at[n], recv_sem=rx.at[n],
+                device_id=(w, g), device_id_type=MESH).wait()
+
+    def add(across, a, n):
+        half = other if across else c
+        at = pl.multiple_of((4 * half + a) * 128, 128)
+        if across:
+            back = xr[a, pl.ds(pl.multiple_of(n * 128, 128), 128), :]
+        else:
+            back = m[a, pl.ds(pl.multiple_of((4 * c + n) * 128, 128), 128), :]
+        n_[n, pl.ds(at, 128), :] = m[n, pl.ds(at, 128), :] + back.T
+
+    def spread(half, a, n, r):
         v = 4 * half + a
         wd = 4 * c + n
-        for r in range(2):
-            gd = 2 * v + r
-            src = n_.at[n, pl.ds(v * 128 + r * KROWS, KROWS), :]
-            dst = o.at[pl.ds(pair * SLOT, KROWS), :]
-
-            @pl.when((gd != g) | (wd != w))
-            def _():
-                pltpu.make_async_remote_copy(
-                    src_ref=src, dst_ref=dst, send_sem=s2.at[n, gd], recv_sem=r2.at[pair],
-                    device_id=(wd, gd), device_id_type=MESH).start()
-
-            @pl.when((gd == g) & (wd == w))
-            def _():
-                pltpu.make_async_copy(src, dst, l2).start()
-                pltpu.make_async_copy(src, dst, l2).wait()
-
-    def own(t, carry):
-        n, a = t // 4, lax.rem(t, 4)
-        at = pl.multiple_of((4 * c + a) * 128, 128)
-        back = pl.multiple_of((4 * c + n) * 128, 128)
-        n_[n, pl.ds(at, 128), :] = m[n, pl.ds(at, 128), :] + m[a, pl.ds(back, 128), :].T
-        spread(n, c, a)
-        return carry
-
-    lax.fori_loop(0, 16, own, 0)
-
-    for n in range(4):
-        pltpu.make_async_remote_copy(
-            src_ref=m.at[n, pl.ds(0, 512), :], dst_ref=xr.at[n], send_sem=sx.at[n], recv_sem=rx.at[n],
-            device_id=(w, g), device_id_type=MESH).wait()
-
-    def cross(t, carry):
-        n, a = t // 4, lax.rem(t, 4)
-        at = pl.multiple_of((4 * other + a) * 128, 128)
-        n_[n, pl.ds(at, 128), :] = m[n, pl.ds(at, 128), :] + xr[a, pl.ds(pl.multiple_of(n * 128, 128), 128), :].T
-        spread(n, other, a)
-        return carry
-
-    lax.fori_loop(0, 16, cross, 0)
+        gd = 2 * v + r
+        src = n_.at[n, pl.ds(v * 128 + r * KROWS, KROWS), :]
+        dst = o.at[pl.ds(pair * SLOT, KROWS), :]
+
+        @pl.when((gd != g) | (wd != w))
+        def _():
+            pltpu.make_async_remote_copy(
+                src_ref=src, dst_ref=dst, send_sem=s2.at[n, gd], recv_sem=r2.at[pair],
+                device_id=(wd, gd), device_id_type=MESH).start()
+
+        @pl.when((gd == g) & (wd == w))
+        def _():
+            pltpu.make_async_copy(src, dst, l2).start()
+            pltpu.make_async_copy(src, dst, l2).wait()
+
+    arrive(0)
+    multiply(0)
+    crossed(0)
+
+    def plain(t, carry):
+        a, n = t // 4, lax.rem(t, 4)
+        add(False, a, n)
+        add(True, a, n)
+        return carry
+
+    pl.semaphore_wait(ready, 7)
+    arrive(1)
+    multiply(1)
+    crossed(1)
+    lax.fori_loop(0, 16, plain, 0)
+    z, x = g // 4, lax.rem(g, 4)
+
+    def out(t, carry):
+        k = lax.rem(t * 11, 64)
+        zd = 2 * lax.rem(k // 32 + c, 2) + lax.rem(k // 16 + z, 2)
+        xd = lax.rem(k // 4 + x, 4)
+        v = 2 * zd + xd // 2
+        spread(zd // 2, lax.rem(v, 4), lax.rem(k + y, 4), lax.rem(xd, 2))
+        return carry
+
+    lax.fori_loop(0, 64, out, 0)
 
     def left1(k, carry):
         q, kk = k // 16, lax.rem(k, 16)
         j = 8 * c + lax.rem(kk // 2 + g, 8)
 
-        @pl.when((j != g) | (q // 2 != c))
+        @pl.when((j != g) | (lax.rem(q, 2) != c))
         def _():
             pltpu.make_async_remote_copy(
                 src_ref=sent.at[0, pl.ds(0, ROWS), :], dst_ref=got.at[0, pl.ds(0, ROWS), :],
@@ -301,7 +322,7 @@
             dma((OWN,)), dma,
             dma((4, 16)), dma((4, 16)), dma((2,)),
             dma((4,)), dma((4,)),
-            dma((4, 16)), dma((PAIRS,)), dma,
+            dma((4, 16)), dma((PAIRS,)), dma, pltpu.SemaphoreType.REGULAR,
         ],
         compiler_params=pltpu.CompilerParams(
             collective_id=0, has_side_effects=True, vmem_limit_bytes=60 * 2**20),

time: 88.4 us -> 73.6 us (0.83)
  the two profiles are of different devices: /device:TPU:25 before, /device:TPU:1 now
where the time goes in v2:
time: 73.6 us; the launch traced here: 73.4 us
  Pallas kernels  70.7 us (96%)
  local copies, waits for them, and re-layouts  2.78 us (4%)
    pallas_call x1, Pallas kernels, on_device(): pl.pallas_call(kernel, out_shape=jax.ShapeDtypeStruct((KROWS, PAIRS, COLS...  70.7 us
    unnamed x1, local copies, waits for them, and re-layouts  2.78 us

profile of v2, /device:TPU:1, one launch (start us, length us, event | category | flops | bytes accessed | tf_op | source)
XLA Modules:
  0.0 73.4 jit_solution(5833726318022089173)
XLA Ops:
  0.0 70.7 %shard_map.28 = f32[50,64,100]{2,1,0:T(8,128)} custom-call(f32[75,8,1200]{2,1,0:T(8,128)} %x_ref.1, f32[800,1200]{1,0:T(8,128)} %bitcast.3), custom_call_target="tpu_custom_call" | custom-call | tf_op jit(solution)/shard_map/pallas_call | solution.py:302
  70.7 2.8 %copy.4 = f32[50,100,64]{1,2,0:T(8,128)} copy(f32[50,100,64]{1,2,0:T(8,128)} %bitcast.2) | data formatting | bytes 2560000

commit v3 on v2

--- a/solution.py
+++ b/solution.py
@@ -20,7 +20,6 @@
 DEPTH = 1280
 COLS = 100
 KROWS = 50
-SLOT = 56
 PAIRS = 64
 
 
@@ -38,7 +37,7 @@
     return dot(ah, bh) + (dot(ah, bl) + dot(al, bh))
 
 
-def kernel(x_ref, ct_ref, out_ref, xbuf, cbuf, th, tl, ch, cl, sent, got, ah, al, m, xr, n_, o,
+def kernel(x_ref, ct_ref, o, xbuf, cbuf, th, tl, fh, fl, ch, cl, sent, sentl, got, gotl, ah, al, m, xr, n_,
            xsem, csem, s1, r1, l1, sx, rx, s2, r2, l2, ready):
     g = lax.axis_index("grp")
     w = lax.axis_index("wide")
@@ -75,17 +74,17 @@
     loads[0].wait()
     lane = lax.broadcasted_iota(jnp.int32, (16, DEPTH), 1)
     row = lax.broadcasted_iota(jnp.int32, (16, DEPTH), 0)
-    for v in range(8):
-        for b in range(7):
-            value = widen(cbuf[pl.ds(COLS * v + 16 * b, 16), :])
-            keep = lane < NAO
-            if b == 6:
-                keep = keep & (row < COLS - 96)
-            hi, lo = split(jnp.where(keep, value, 0.0))
-            ch[pl.ds(128 * v + 16 * b, 16), :] = hi
-            cl[pl.ds(128 * v + 16 * b, 16), :] = lo
-        ch[pl.ds(128 * v + 112, 16), :] = jnp.zeros((16, DEPTH), BF16)
-        cl[pl.ds(128 * v + 112, 16), :] = jnp.zeros((16, DEPTH), BF16)
+
+    def flat(b, carry):
+        at = pl.multiple_of(16 * b, 16)
+        hi, lo = split(widen(cbuf[pl.ds(at, 16), :]))
+        fh[pl.ds(at, 16), :] = hi
+        fl[pl.ds(at, 16), :] = lo
+        return carry
+
+    lax.fori_loop(0, 50, flat, 0)
+    fh[pl.ds(800, 112), :] = jnp.zeros((112, DEPTH), BF16)
+    fl[pl.ds(800, 112), :] = jnp.zeros((112, DEPTH), BF16)
 
     for p in range(OWN):
         loads[1 + p].wait()
@@ -106,44 +105,59 @@
     for n in range(4):
         got[n, pl.ds(NAO, DEPTH - NAO), :] = jnp.zeros((DEPTH - NAO, 128), F32)
 
-    pl.semaphore_wait(barrier, 16 + 7 - jnp.where(src1 == c, 1, 0))
-
-    def pass_on(d, carry):
-        @pl.when(d != w)
-        def _():
-            pl.semaphore_signal(ready, inc=1, device_id=(d, g), device_id_type=MESH)
-        return carry
-
-    lax.fori_loop(0, 8, pass_on, 0)
+    narrow = lax.broadcasted_iota(jnp.int32, (8, 128), 1) < 16
 
     def stage1(q, carry):
         c2, h = lax.rem(q, 2), q // 2
-        base = pl.multiple_of(c2 * 512 + h * 256, 256)
-        bh = ch[pl.ds(base, 256), :]
-        bl = cl[pl.ds(base, 256), :]
-        acc = dot3(th[...], tl[...], bh, bl, NT)
-        for e in range(2):
-            sent[2 * q + e] = acc[:, 128 * e:128 * (e + 1)]
+        base = pl.multiple_of(c2 * 400 + h * 256, 16)
+        acc = dot3(th[...], tl[...], fh[pl.ds(base, 256), :], fl[pl.ds(base, 256), :], NT)
+        sent[2 * q] = acc[:, :128]
+
+        @pl.when(h == 0)
+        def _():
+            sent[2 * q + 1] = acc[:, 128:]
+
+        @pl.when(h == 1)
+        def _():
+            for i in range(OWN):
+                parts = [jnp.where(narrow, acc[BAND * i + 8 * b:BAND * i + 8 * b + 8, 128:], 0.0) for b in range(10)]
+                first = parts[0]
+                for b in range(1, 8):
+                    first = first + pltpu.roll(parts[b], 16 * b, 1)
+                sentl[c2, pl.ds(16 * i, 8), :] = first
+                sentl[c2, pl.ds(16 * i + 8, 8), :] = parts[8] + pltpu.roll(parts[9], 16, 1)
+
+        @pl.when(q == 0)
+        def _():
+            pl.semaphore_wait(barrier, 16 + 7 - jnp.where(src1 == c, 1, 0))
+
         wd = y * 2 + c2
+
+        def put(src, dst, j, k, tile):
+            @pl.when((j != g) | (c2 != c))
+            def _():
+                pltpu.make_async_remote_copy(
+                    src_ref=src, dst_ref=dst, send_sem=s1.at[q, k], recv_sem=r1.at[tile, g],
+                    device_id=(wd, j), device_id_type=MESH).start()
+
+            @pl.when((j == g) & (c2 == c))
+            def _():
+                pltpu.make_async_copy(src, dst, l1).start()
+                pltpu.make_async_copy(src, dst, l1).wait()
 
         def send(k, carry):
             i = lax.rem(k // 2 + g, 8)
             e = lax.rem(k, 2)
             j = 8 * c + i
             tile = 2 * h + e
-            src = sent.at[2 * q + e, pl.ds(i * BAND, ROWS), :]
-            dst = got.at[tile, pl.ds(ROWS * g, ROWS), :]
-
-            @pl.when((j != g) | (c2 != c))
+
+            @pl.when(tile < 3)
             def _():
-                pltpu.make_async_remote_copy(
-                    src_ref=src, dst_ref=dst, send_sem=s1.at[q, k], recv_sem=r1.at[tile, g],
-                    device_id=(wd, j), device_id_type=MESH).start()
-
-            @pl.when((j == g) & (c2 == c))
+                put(sent.at[2 * q + e, pl.ds(i * BAND, ROWS), :], got.at[tile, pl.ds(ROWS * g, ROWS), :], j, k, tile)
+
+            @pl.when(tile == 3)
             def _():
-                pltpu.make_async_copy(src, dst, l1.at[e]).start()
-                pltpu.make_async_copy(src, dst, l1.at[e]).wait()
+                put(sentl.at[c2, pl.ds(16 * i, 16), :], gotl.at[pl.ds(16 * g, 16), :], j, k, tile)
             return carry
 
         lax.fori_loop(0, 16, send, 0)
@@ -151,26 +165,62 @@
 
     lax.fori_loop(0, 4, stage1, 0)
 
+    def pass_on(d, carry):
+        @pl.when(d != w)
+        def _():
+            pl.semaphore_signal(ready, inc=1, device_id=(d, g), device_id_type=MESH)
+        return carry
+
+    lax.fori_loop(0, 8, pass_on, 0)
+
+    for v in range(8):
+        for b in range(7):
+            value = widen(cbuf[pl.ds(COLS * v + 16 * b, 16), :])
+            if b == 6:
+                value = jnp.where(row < COLS - 96, value, 0.0)
+            hi, lo = split(value)
+            ch[pl.ds(128 * v + 16 * b, 16), :] = hi
+            cl[pl.ds(128 * v + 16 * b, 16), :] = lo
+        ch[pl.ds(128 * v + 112, 16), :] = jnp.zeros((16, DEPTH), BF16)
+        cl[pl.ds(128 * v + 112, 16), :] = jnp.zeros((16, DEPTH), BF16)
+
     pair = 16 * y + g
 
     def arrive(h):
-        def one(k, carry):
-            tile, gs = 2 * h + k // 16, lax.rem(k, 16)
-
-            @pl.when((gs != g) | (src1 != c))
-            def _():
-                pltpu.make_async_remote_copy(
-                    src_ref=sent.at[0, pl.ds(0, ROWS), :], dst_ref=got.at[tile, pl.ds(ROWS * gs, ROWS), :],
-                    send_sem=s1.at[0, 0], recv_sem=r1.at[tile, gs], device_id=(w, g), device_id_type=MESH).wait_recv()
-            return carry
-
-        lax.fori_loop(0, 32, one, 0)
+        for tile in (2 * h, 2 * h + 1):
+            def one(gs, carry):
+                @pl.when((gs != g) | (src1 != c))
+                def _():
+                    if tile < 3:
+                        src, dst = sent.at[0, pl.ds(0, ROWS), :], got.at[tile, pl.ds(ROWS * gs, ROWS), :]
+                    else:
+                        src, dst = sentl.at[0, pl.ds(0, 16), :], gotl.at[pl.ds(16 * gs, 16), :]
+                    pltpu.make_async_remote_copy(
+                        src_ref=src, dst_ref=dst, send_sem=s1.at[0, 0], recv_sem=r1.at[tile, gs],
+                        device_id=(w, g), device_id_type=MESH).wait_recv()
+                return carry
+
+            lax.fori_loop(0, 16, one, 0)
 
     def multiply(h):
+        if h == 1:
+            for gs in range(16):
+                for b in range(10):
+                    part = gotl[pl.ds(16 * gs + 8 * (b // 8), 8), :]
+                    if b % 8:
+                        part = pltpu.roll(part, 128 - 16 * (b % 8), 1)
+                    got[3, pl.ds(ROWS * gs + 8 * b, 8), :] = part
+
         def halves(b, carry):
             at = pl.multiple_of(b * 128, 128)
+            here = lax.broadcasted_iota(jnp.int32, (128, 128), 1)
             for e in range(2):
-                hi, lo = split(got[2 * h + e, pl.ds(at, 128), :])
+                n = 2 * h + e
+                value = got[n, pl.ds(at, 128), :]
+                if n:
+                    before = got[n - 1, pl.ds(at, 128), :]
+                    value = jnp.where(here < 28 * n, pltpu.roll(before, 28 * n, 1), pltpu.roll(value, 28 * n, 1))
+                hi, lo = split(value)
                 ah[pl.ds(at, 128), pl.ds(128 * e, 128)] = hi
                 al[pl.ds(at, 128), pl.ds(128 * e, 128)] = lo
             return carry
@@ -214,7 +264,7 @@
         wd = 4 * c + n
         gd = 2 * v + r
         src = n_.at[n, pl.ds(v * 128 + r * KROWS, KROWS), :]
-        dst = o.at[pl.ds(pair * SLOT, KROWS), :]
+        dst = o.at[:, pair, :]
 
         @pl.when((gd != g) | (wd != w))
         def _():
@@ -230,26 +280,32 @@
     arrive(0)
     multiply(0)
     crossed(0)
-
-    def plain(t, carry):
-        a, n = t // 4, lax.rem(t, 4)
-        add(False, a, n)
-        add(True, a, n)
-        return carry
 
     pl.semaphore_wait(ready, 7)
     arrive(1)
     multiply(1)
     crossed(1)
-    lax.fori_loop(0, 16, plain, 0)
     z, x = g // 4, lax.rem(g, 4)
 
     def out(t, carry):
         k = lax.rem(t * 11, 64)
         zd = 2 * lax.rem(k // 32 + c, 2) + lax.rem(k // 16 + z, 2)
         xd = lax.rem(k // 4 + x, 4)
-        v = 2 * zd + xd // 2
-        spread(zd // 2, lax.rem(v, 4), lax.rem(k + y, 4), lax.rem(xd, 2))
+        n = lax.rem(k + y, 4)
+        half, r = zd // 2, lax.rem(xd, 2)
+        a = 2 * lax.rem(zd, 2) + xd // 2
+        twin = 16 * (k // 16) + 4 * lax.rem(xd + 1 - 2 * r + 4 - x, 4) + lax.rem(k, 4)
+        first = t < lax.rem(twin * 35, 64)
+
+        @pl.when(first & (half == c))
+        def _():
+            add(False, a, n)
+
+        @pl.when(first & (half != c))
+        def _():
+            add(True, a, n)
+
+        spread(half, a, n, r)
         return carry
 
     lax.fori_loop(0, 64, out, 0)
@@ -257,12 +313,21 @@
     def left1(k, carry):
         q, kk = k // 16, lax.rem(k, 16)
         j = 8 * c + lax.rem(kk // 2 + g, 8)
-
-        @pl.when((j != g) | (lax.rem(q, 2) != c))
-        def _():
+        last = (q >= 2) & (lax.rem(kk, 2) == 1)
+        moved = (j != g) | (lax.rem(q, 2) != c)
+
+        def gone(src):
             pltpu.make_async_remote_copy(
-                src_ref=sent.at[0, pl.ds(0, ROWS), :], dst_ref=got.at[0, pl.ds(0, ROWS), :],
-                send_sem=s1.at[q, kk], recv_sem=r1.at[0, 0], device_id=(w, g), device_id_type=MESH).wait_send()
+                src_ref=src, dst_ref=src, send_sem=s1.at[q, kk], recv_sem=r1.at[0, 0],
+                device_id=(w, g), device_id_type=MESH).wait_send()
+
+        @pl.when(moved & jnp.logical_not(last))
+        def _():
+            gone(sent.at[0, pl.ds(0, ROWS), :])
+
+        @pl.when(moved & last)
+        def _():
+            gone(sentl.at[0, pl.ds(0, 16), :])
         return carry
 
     lax.fori_loop(0, 64, left1, 0)
@@ -273,7 +338,7 @@
         @pl.when((gd != g) | (4 * c + n != w))
         def _():
             pltpu.make_async_remote_copy(
-                src_ref=n_.at[0, pl.ds(0, KROWS), :], dst_ref=o.at[pl.ds(0, KROWS), :],
+                src_ref=n_.at[0, pl.ds(0, KROWS), :], dst_ref=o.at[:, 0, :],
                 send_sem=s2.at[n, gd], recv_sem=r2.at[0], device_id=(w, g), device_id_type=MESH).wait_send()
         return carry
 
@@ -283,50 +348,51 @@
         @pl.when((q != pair) | (src2 != c))
         def _():
             pltpu.make_async_remote_copy(
-                src_ref=n_.at[0, pl.ds(0, KROWS), :], dst_ref=o.at[pl.ds(q * SLOT, KROWS), :],
+                src_ref=n_.at[0, pl.ds(0, KROWS), :], dst_ref=o.at[:, q, :],
                 send_sem=s2.at[0, 0], recv_sem=r2.at[q], device_id=(w, g), device_id_type=MESH).wait_recv()
         return carry
 
     lax.fori_loop(0, PAIRS, landed, 0)
 
-    def gather(k, carry):
-        for b in range(PAIRS // 8):
-            out_ref[k, pl.ds(8 * b, 8), :] = o[pl.ds(8 * b * SLOT + k, 8, stride=SLOT), :][:, :COLS]
-        return carry
-
-    lax.fori_loop(0, KROWS, gather, 0)
+
+def arrange(o_ref, out_ref):
+    out_ref[...] = o_ref[:, :, :COLS]
 
 
 def on_device(integrals, coeffs):
     dma = pltpu.SemaphoreType.DMA
-    slab = pl.pallas_call(
+    blocks = pl.pallas_call(
         kernel,
-        out_shape=jax.ShapeDtypeStruct((KROWS, PAIRS, COLS), F32),
+        out_shape=jax.ShapeDtypeStruct((KROWS, PAIRS, 128), F32),
         in_specs=[pl.BlockSpec(memory_space=pl.ANY)] * 2,
-        out_specs=pl.BlockSpec(memory_space=pltpu.VMEM),
+        out_specs=pl.BlockSpec(memory_space=pl.ANY),
         scratch_shapes=[
             pltpu.VMEM((OWN, ROWS, NAO), F32),
             pltpu.VMEM((816, NAO), F32),
             pltpu.VMEM((OWN * BAND, DEPTH), BF16),
             pltpu.VMEM((OWN * BAND, DEPTH), BF16),
+            pltpu.VMEM((912, DEPTH), BF16),
+            pltpu.VMEM((912, DEPTH), BF16),
             pltpu.VMEM((1024, DEPTH), BF16),
             pltpu.VMEM((1024, DEPTH), BF16),
             pltpu.VMEM((8, OWN * BAND, 128), F32),
+            pltpu.VMEM((2, OWN * 16, 128), F32),
             pltpu.VMEM((4, DEPTH, 128), F32),
+            pltpu.VMEM((256, 128), F32),
             pltpu.VMEM((DEPTH, 256), BF16),
             pltpu.VMEM((DEPTH, 256), BF16),
             pltpu.VMEM((4, 1024, 128), F32),
             pltpu.VMEM((4, 512, 128), F32),
             pltpu.VMEM((4, 1024, 128), F32),
-            pltpu.VMEM((PAIRS * SLOT, 128), F32),
             dma((OWN,)), dma,
-            dma((4, 16)), dma((4, 16)), dma((2,)),
+            dma((4, 16)), dma((4, 16)), dma,
             dma((4,)), dma((4,)),
             dma((4, 16)), dma((PAIRS,)), dma, pltpu.SemaphoreType.REGULAR,
         ],
         compiler_params=pltpu.CompilerParams(
             collective_id=0, has_side_effects=True, vmem_limit_bytes=60 * 2**20),
     )(integrals, coeffs.T)
+    slab = blocks[:, :, :COLS]
     return jnp.transpose(slab, (0, 2, 1))
 
 

time: 73.6 us -> 67.3 us (0.914)
  Pallas kernels: 70.7 us -> 64.4 us
    pallas_call x1, Pallas kernels: 70.7 us -> 64.4 us  [on_device(): pl.pallas_call(kernel, out_shape=jax.ShapeDtypeStruct((KROWS, PAIRS, 128)...]
    transpose x0 -> x1, local copies, waits for them, and re-layouts: none -> 2.78 us  [on_device(): return jnp.transpose(slab, (0, 2, 1))]
    unnamed x1 -> x0, local copies, waits for them, and re-layouts: 2.78 us -> none
where the time goes in v3:
time: 67.3 us; the launch traced here: 67.2 us
  Pallas kernels  64.4 us (96%)
  local copies, waits for them, and re-layouts  2.78 us (4%)
    pallas_call x1, Pallas kernels, on_device(): pl.pallas_call(kernel, out_shape=jax.ShapeDtypeStruct((KROWS, PAIRS, 128)...  64.4 us
    transpose x1, local copies, waits for them, and re-layouts, on_device(): return jnp.transpose(slab, (0, 2, 1))  2.78 us

profile of v3, /device:TPU:1, one launch (start us, length us, event | category | flops | bytes accessed | tf_op | source)
XLA Modules:
  0.0 67.2 jit_solution(3553217337001127966)
XLA Ops:
  0.0 64.4 %shard_map.28 = f32[50,64,128]{2,1,0:T(8,128)} custom-call(f32[75,8,1200]{2,1,0:T(8,128)} %x_ref.1, f32[800,1200]{1,0:T(8,128)} %bitcast.3), custom_call_target="tpu_custom_call" | custom-call | tf_op jit(solution)/shard_map/pallas_call | solution.py:364
  64.4 2.8 %slice_bitcast_fusion = f32[50,100,64]{1,2,0:T(8,128)} fusion(f32[50,64,128]{2,1,0:T(8,128)} %shard_map.28), kind=kLoop, calls=%fused_computation | loop fusion | bytes 2560000 | tf_op jit(solution)/shard_map/transpose | solution.py:396

commit v4 on v3

--- a/solution.py
+++ b/solution.py
@@ -21,6 +21,8 @@
 COLS = 100
 KROWS = 50
 PAIRS = 64
+SENT = 42
+SLOT = 48
 
 
 def split(v):
@@ -37,7 +39,7 @@
     return dot(ah, bh) + (dot(ah, bl) + dot(al, bh))
 
 
-def kernel(x_ref, ct_ref, o, xbuf, cbuf, th, tl, fh, fl, ch, cl, sent, sentl, got, gotl, ah, al, m, xr, n_,
+def kernel(x_ref, ct_ref, o, xbuf, cbuf, th, tl, fh, fl, ch, cl, sent, sentl, got, gotl, ah, al, m, xr, whole, n_,
            xsem, csem, s1, r1, l1, sx, rx, s2, r2, l2, ready):
     g = lax.axis_index("grp")
     w = lax.axis_index("wide")
@@ -250,6 +252,8 @@
                 src_ref=m.at[n, pl.ds(0, 512), :], dst_ref=xr.at[n], send_sem=sx.at[n], recv_sem=rx.at[n],
                 device_id=(w, g), device_id_type=MESH).wait()
 
+    main = lax.broadcasted_iota(jnp.int32, (8, 128), 1) < COLS
+
     def add(across, a, n):
         half = other if across else c
         at = pl.multiple_of((4 * half + a) * 128, 128)
@@ -257,14 +261,21 @@
             back = xr[a, pl.ds(pl.multiple_of(n * 128, 128), 128), :]
         else:
             back = m[a, pl.ds(pl.multiple_of((4 * c + n) * 128, 128), 128), :]
-        n_[n, pl.ds(at, 128), :] = m[n, pl.ds(at, 128), :] + back.T
+        whole[...] = m[n, pl.ds(at, 128), :] + back.T
+        for r in range(2):
+            slot = 2 * (4 * half + a) + r
+            rest = whole[pl.ds(KROWS * r + SENT, 8), :]
+            for j in range(4):
+                n_[n, slot, pl.ds(8 * j, 8), :] = jnp.where(
+                    main, whole[pl.ds(KROWS * r + 8 * j, 8), :], pltpu.roll(rest, COLS - 25 * j, 1))
+            n_[n, slot, pl.ds(32, SENT - 32), :] = whole[pl.ds(KROWS * r + 32, SENT - 32), :]
 
     def spread(half, a, n, r):
         v = 4 * half + a
         wd = 4 * c + n
         gd = 2 * v + r
-        src = n_.at[n, pl.ds(v * 128 + r * KROWS, KROWS), :]
-        dst = o.at[:, pair, :]
+        src = n_.at[n, gd, pl.ds(0, SENT), :]
+        dst = o.at[pl.ds(pair * SLOT, SENT), :]
 
         @pl.when((gd != g) | (wd != w))
         def _():
@@ -338,7 +349,7 @@
         @pl.when((gd != g) | (4 * c + n != w))
         def _():
             pltpu.make_async_remote_copy(
-                src_ref=n_.at[0, pl.ds(0, KROWS), :], dst_ref=o.at[:, 0, :],
+                src_ref=n_.at[0, 0, pl.ds(0, SENT), :], dst_ref=o.at[pl.ds(0, SENT), :],
                 send_sem=s2.at[n, gd], recv_sem=r2.at[0], device_id=(w, g), device_id_type=MESH).wait_send()
         return carry
 
@@ -348,7 +359,7 @@
         @pl.when((q != pair) | (src2 != c))
         def _():
             pltpu.make_async_remote_copy(
-                src_ref=n_.at[0, pl.ds(0, KROWS), :], dst_ref=o.at[:, q, :],
+                src_ref=n_.at[0, 0, pl.ds(0, SENT), :], dst_ref=o.at[pl.ds(q * SLOT, SENT), :],
                 send_sem=s2.at[0, 0], recv_sem=r2.at[q], device_id=(w, g), device_id_type=MESH).wait_recv()
         return carry
 
@@ -356,14 +367,32 @@
 
 
 def arrange(o_ref, out_ref):
-    out_ref[...] = o_ref[:, :, :COLS]
+    def plain(k, carry):
+        for b in range(PAIRS // 8):
+            out_ref[k, pl.ds(8 * b, 8), :] = o_ref[pl.ds(8 * b * SLOT + k, 8, stride=SLOT), :][:, :COLS]
+        return carry
+
+    lax.fori_loop(0, SENT, plain, 0, unroll=6)
+    lane = lax.broadcasted_iota(jnp.int32, (8, 128), 1)
+
+    def parts(q, carry):
+        for b in range(PAIRS // 8):
+            value = jnp.zeros((8, 128), F32)
+            for j in range(4):
+                part = o_ref[pl.ds(8 * b * SLOT + 8 * j + q, 8, stride=SLOT), :]
+                part = pltpu.roll(part, 28 + 25 * j, 1)
+                value = part if j == 0 else jnp.where(lane >= 25 * j, part, value)
+            out_ref[SENT + q, pl.ds(8 * b, 8), :] = value[:, :COLS]
+        return carry
+
+    lax.fori_loop(0, 8, parts, 0, unroll=2)
 
 
 def on_device(integrals, coeffs):
     dma = pltpu.SemaphoreType.DMA
     blocks = pl.pallas_call(
         kernel,
-        out_shape=jax.ShapeDtypeStruct((KROWS, PAIRS, 128), F32),
+        out_shape=jax.ShapeDtypeStruct((PAIRS * SLOT, 128), F32),
         in_specs=[pl.BlockSpec(memory_space=pl.ANY)] * 2,
         out_specs=pl.BlockSpec(memory_space=pl.ANY),
         scratch_shapes=[
@@ -383,7 +412,8 @@
             pltpu.VMEM((DEPTH, 256), BF16),
             pltpu.VMEM((4, 1024, 128), F32),
             pltpu.VMEM((4, 512, 128), F32),
-            pltpu.VMEM((4, 1024, 128), F32),
+            pltpu.VMEM((128, 128), F32),
+            pltpu.VMEM((4, 16, SLOT, 128), F32),
             dma((OWN,)), dma,
             dma((4, 16)), dma((4, 16)), dma,
             dma((4,)), dma((4,)),
@@ -392,7 +422,12 @@
         compiler_params=pltpu.CompilerParams(
             collective_id=0, has_side_effects=True, vmem_limit_bytes=60 * 2**20),
     )(integrals, coeffs.T)
-    slab = blocks[:, :, :COLS]
+    slab = pl.pallas_call(
+        arrange,
+        out_shape=jax.ShapeDtypeStruct((KROWS, PAIRS, COLS), F32),
+        in_specs=[pl.BlockSpec(memory_space=pltpu.VMEM)],
+        out_specs=pl.BlockSpec(memory_space=pltpu.VMEM),
+    )(blocks)
     return jnp.transpose(slab, (0, 2, 1))
 
 

time: 67.3 us -> 65.5 us (0.973)
  local copies, waits for them, and re-layouts: 2.78 us -> 0 us
  Pallas kernels: 64.4 us -> 65.3 us
    transpose x1 -> x0, local copies, waits for them, and re-layouts: 2.78 us -> none  [on_device(): return jnp.transpose(slab, (0, 2, 1))]
    pallas_call x1 -> x2, Pallas kernels: 64.4 us -> 65.3 us  [the longest x1 61.7 us: on_device(): pl.pallas_call(kernel, out_shape=jax.ShapeDtypeStruct((PAIRS * SLOT, 128)...]
where the time goes in v4:
time: 65.5 us; the launch traced here: 65.3 us
  Pallas kernels  65.3 us (100%)
    pallas_call x1, Pallas kernels, on_device(): pl.pallas_call(kernel, out_shape=jax.ShapeDtypeStruct((PAIRS * SLOT, 128)...  61.7 us
    pallas_call x1, Pallas kernels, on_device(): pl.pallas_call(arrange, out_shape=jax.ShapeDtypeStruct((KROWS, PAIRS, COL...  3.61 us

profile of v4, /device:TPU:1, one launch (start us, length us, event | category | flops | bytes accessed | tf_op | source)
XLA Modules:
  0.0 65.3 jit_solution(13777304058749412914)
XLA Ops:
  0.0 61.7 %shard_map.28.o_ref = f32[3072,128]{1,0:T(8,128)} custom-call(f32[75,8,1200]{2,1,0:T(8,128)} %x_ref.1, f32[800,1200]{1,0:T(8,128)} %bitcast.2), custom_call_target="tpu_custom_call" | custom-call | tf_op jit(solution)/shard_map/pallas_call | solution.py:393
  61.7 3.6 %shard_map.29 = f32[50,64,100]{2,1,0:T(8,128)} custom-call(f32[3072,128]{1,0:T(8,128)} %shard_map.28.o_ref), custom_call_target="tpu_custom_call" | custom-call | tf_op jit(solution)/shard_map/pallas_call | solution.py:425

commit v5 on v4

--- a/solution.py
+++ b/solution.py
@@ -39,7 +39,7 @@
     return dot(ah, bh) + (dot(ah, bl) + dot(al, bh))
 
 
-def kernel(x_ref, ct_ref, o, xbuf, cbuf, th, tl, fh, fl, ch, cl, sent, sentl, got, gotl, ah, al, m, xr, whole, n_,
+def kernel(x_ref, ct_ref, o, xbuf, cbuf, th, tl, fh, fl, sent, sentl, got, gotl, ah, al, product, m, xr, whole, n_,
            xsem, csem, s1, r1, l1, sx, rx, s2, r2, l2, ready):
     g = lax.axis_index("grp")
     w = lax.axis_index("wide")
@@ -47,7 +47,7 @@
     other = 1 - c
     barrier = pltpu.get_barrier_semaphore()
 
-    loads = [pltpu.make_async_copy(ct_ref, cbuf.at[pl.ds(0, 800), :], csem)]
+    loads = [pltpu.make_async_copy(ct_ref, cbuf, csem)]
     for p in range(OWN):
         loads.append(pltpu.make_async_copy(x_ref.at[:, p, :], xbuf.at[p], xsem.at[p]))
     for load in loads:
@@ -148,8 +148,8 @@
                 pltpu.make_async_copy(src, dst, l1).wait()
 
         def send(k, carry):
-            i = lax.rem(k // 2 + g, 8)
-            e = lax.rem(k, 2)
+            i = lax.rem(jnp.where(h == 0, k // 2, k) + g, 8)
+            e = jnp.where(h == 0, lax.rem(k, 2), 1 - k // 8)
             j = 8 * c + i
             tile = 2 * h + e
 
@@ -175,21 +175,14 @@
 
     lax.fori_loop(0, 8, pass_on, 0)
 
-    for v in range(8):
-        for b in range(7):
-            value = widen(cbuf[pl.ds(COLS * v + 16 * b, 16), :])
-            if b == 6:
-                value = jnp.where(row < COLS - 96, value, 0.0)
-            hi, lo = split(value)
-            ch[pl.ds(128 * v + 16 * b, 16), :] = hi
-            cl[pl.ds(128 * v + 16 * b, 16), :] = lo
-        ch[pl.ds(128 * v + 112, 16), :] = jnp.zeros((16, DEPTH), BF16)
-        cl[pl.ds(128 * v + 112, 16), :] = jnp.zeros((16, DEPTH), BF16)
+    for n in range(4):
+        for v in range(8):
+            m[n, pl.ds(128 * v + COLS, 128 - COLS), :] = jnp.zeros((128 - COLS, 128), F32)
 
     pair = 16 * y + g
 
-    def arrive(h):
-        for tile in (2 * h, 2 * h + 1):
+    def arrive(*tiles):
+        for tile in tiles:
             def one(gs, carry):
                 @pl.when((gs != g) | (src1 != c))
                 def _():
@@ -205,14 +198,6 @@
             lax.fori_loop(0, 16, one, 0)
 
     def multiply(h):
-        if h == 1:
-            for gs in range(16):
-                for b in range(10):
-                    part = gotl[pl.ds(16 * gs + 8 * (b // 8), 8), :]
-                    if b % 8:
-                        part = pltpu.roll(part, 128 - 16 * (b % 8), 1)
-                    got[3, pl.ds(ROWS * gs + 8 * b, 8), :] = part
-
         def halves(b, carry):
             at = pl.multiple_of(b * 128, 128)
             here = lax.broadcasted_iota(jnp.int32, (128, 128), 1)
@@ -230,10 +215,13 @@
         lax.fori_loop(0, DEPTH // 128, halves, 0)
 
         def rows_of(half, carry):
-            at = pl.multiple_of(lax.rem(half + other, 2) * 512, 512)
-            acc = dot3(ch[pl.ds(at, 512), :], cl[pl.ds(at, 512), :], ah[...], al[...], NN)
-            for e in range(2):
-                m[2 * h + e, pl.ds(at, 512), :] = acc[:, 128 * e:128 * (e + 1)]
+            side = lax.rem(half + other, 2)
+            at = pl.multiple_of(side * 512, 512)
+            mine = pl.ds(pl.multiple_of(side * 400, 16), 400)
+            product[...] = dot3(fh[mine, :], fl[mine, :], ah[...], al[...], NN)
+            for a in range(4):
+                for e in range(2):
+                    m[2 * h + e, pl.ds(at + 128 * a, COLS), :] = product[pl.ds(COLS * a, COLS), pl.ds(128 * e, 128)]
 
             @pl.when(half == 0)
             def _():
@@ -288,14 +276,27 @@
             pltpu.make_async_copy(src, dst, l2).start()
             pltpu.make_async_copy(src, dst, l2).wait()
 
-    arrive(0)
+    arrive(0, 1)
     multiply(0)
     crossed(0)
 
+    def quarter(t, carry):
+        add(False, t // 2, lax.rem(t, 2))
+        add(True, t // 2, lax.rem(t, 2))
+        return carry
+
+    lax.fori_loop(0, 4, quarter, 0)
+
     pl.semaphore_wait(ready, 7)
-    arrive(1)
+    arrive(3)
+    for gs in range(16):
+        for b in range(10):
+            part = gotl[pl.ds(16 * gs + 8 * (b // 8), 8), :]
+            if b % 8:
+                part = pltpu.roll(part, 128 - 16 * (b % 8), 1)
+            got[3, pl.ds(ROWS * gs + 8 * b, 8), :] = part
+    arrive(2)
     multiply(1)
-    crossed(1)
     z, x = g // 4, lax.rem(g, 4)
 
     def out(t, carry):
@@ -306,7 +307,11 @@
         half, r = zd // 2, lax.rem(xd, 2)
         a = 2 * lax.rem(zd, 2) + xd // 2
         twin = 16 * (k // 16) + 4 * lax.rem(xd + 1 - 2 * r + 4 - x, 4) + lax.rem(k, 4)
-        first = t < lax.rem(twin * 35, 64)
+        first = ((a > 1) | (n > 1)) & (t < lax.rem(twin * 35, 64))
+
+        @pl.when(t == 3)
+        def _():
+            crossed(1)
 
         @pl.when(first & (half == c))
         def _():
@@ -323,8 +328,8 @@
 
     def left1(k, carry):
         q, kk = k // 16, lax.rem(k, 16)
-        j = 8 * c + lax.rem(kk // 2 + g, 8)
-        last = (q >= 2) & (lax.rem(kk, 2) == 1)
+        j = 8 * c + lax.rem(jnp.where(q < 2, kk // 2, kk) + g, 8)
+        last = (q >= 2) & (kk < 8)
         moved = (j != g) | (lax.rem(q, 2) != c)
 
         def gone(src):
@@ -392,24 +397,23 @@
     dma = pltpu.SemaphoreType.DMA
     blocks = pl.pallas_call(
         kernel,
-        out_shape=jax.ShapeDtypeStruct((PAIRS * SLOT, 128), F32),
+        out_shape=jax.ShapeDtypeStruct(((PAIRS + 1) * SLOT, 128), F32),
         in_specs=[pl.BlockSpec(memory_space=pl.ANY)] * 2,
         out_specs=pl.BlockSpec(memory_space=pl.ANY),
         scratch_shapes=[
             pltpu.VMEM((OWN, ROWS, NAO), F32),
-            pltpu.VMEM((816, NAO), F32),
+            pltpu.VMEM((800, NAO), F32),
             pltpu.VMEM((OWN * BAND, DEPTH), BF16),
             pltpu.VMEM((OWN * BAND, DEPTH), BF16),
             pltpu.VMEM((912, DEPTH), BF16),
             pltpu.VMEM((912, DEPTH), BF16),
-            pltpu.VMEM((1024, DEPTH), BF16),
-            pltpu.VMEM((1024, DEPTH), BF16),
             pltpu.VMEM((8, OWN * BAND, 128), F32),
             pltpu.VMEM((2, OWN * 16, 128), F32),
             pltpu.VMEM((4, DEPTH, 128), F32),
             pltpu.VMEM((256, 128), F32),
             pltpu.VMEM((DEPTH, 256), BF16),
             pltpu.VMEM((DEPTH, 256), BF16),
+            pltpu.VMEM((400, 256), F32),
             pltpu.VMEM((4, 1024, 128), F32),
             pltpu.VMEM((4, 512, 128), F32),
             pltpu.VMEM((128, 128), F32),
@@ -420,13 +424,14 @@
             dma((4, 16)), dma((PAIRS,)), dma, pltpu.SemaphoreType.REGULAR,
         ],
         compiler_params=pltpu.CompilerParams(
-            collective_id=0, has_side_effects=True, vmem_limit_bytes=60 * 2**20),
+            collective_id=0, has_side_effects=True, vmem_limit_bytes=51 * 2**20),
     )(integrals, coeffs.T)
     slab = pl.pallas_call(
         arrange,
         out_shape=jax.ShapeDtypeStruct((KROWS, PAIRS, COLS), F32),
         in_specs=[pl.BlockSpec(memory_space=pltpu.VMEM)],
         out_specs=pl.BlockSpec(memory_space=pltpu.VMEM),
+        compiler_params=pltpu.CompilerParams(vmem_limit_bytes=16 * 2**20),
     )(blocks)
     return jnp.transpose(slab, (0, 2, 1))
 

time: 65.5 us -> 62.4 us (0.953)
  Pallas kernels: 65.3 us -> 62.3 us
    pallas_call x1, Pallas kernels: 61.7 us -> 60.1 us  [on_device(): pl.pallas_call(kernel, out_shape=jax.ShapeDtypeStruct(((PAIRS + 1) * SLOT...]
    pallas_call x1, Pallas kernels: 3.61 us -> 2.21 us  [on_device(): pl.pallas_call(arrange, out_shape=jax.ShapeDtypeStruct((KROWS, PAIRS, COL...]
where the time goes in v5:
time: 62.4 us; the launch traced here: 62.3 us
  Pallas kernels  62.3 us (100%)
    pallas_call x1, Pallas kernels, on_device(): pl.pallas_call(kernel, out_shape=jax.ShapeDtypeStruct(((PAIRS + 1) * SLOT...  60.1 us
    pallas_call x1, Pallas kernels, on_device(): pl.pallas_call(arrange, out_shape=jax.ShapeDtypeStruct((KROWS, PAIRS, COL...  2.21 us

profile of v5, /device:TPU:1, one launch (start us, length us, event | category | flops | bytes accessed | tf_op | source)
XLA Modules:
  0.0 62.3 jit_solution(14113592879709350986)
XLA Ops:
  0.0 60.1 %shard_map.28.o_ref = f32[3120,128]{1,0:T(8,128)S(1)} custom-call(f32[75,8,1200]{2,1,0:T(8,128)} %x_ref.1, f32[800,1200]{1,0:T(8,128)} %bitcast.2), custom_call_target="tpu_custom_call" | custom-call | tf_op jit(solution)/shard_map/pallas_call | solution.py:398
  60.1 2.2 %shard_map.29 = f32[50,64,100]{2,1,0:T(8,128)} custom-call(f32[3120,128]{1,0:T(8,128)S(1)} %shard_map.28.o_ref), custom_call_target="tpu_custom_call" | custom-call | tf_op jit(solution)/shard_map/pallas_call | solution.py:429

commit v6 on v5

--- a/solution.py
+++ b/solution.py
@@ -77,14 +77,6 @@
     lane = lax.broadcasted_iota(jnp.int32, (16, DEPTH), 1)
     row = lax.broadcasted_iota(jnp.int32, (16, DEPTH), 0)
 
-    def flat(b, carry):
-        at = pl.multiple_of(16 * b, 16)
-        hi, lo = split(widen(cbuf[pl.ds(at, 16), :]))
-        fh[pl.ds(at, 16), :] = hi
-        fl[pl.ds(at, 16), :] = lo
-        return carry
-
-    lax.fori_loop(0, 50, flat, 0)
     fh[pl.ds(800, 112), :] = jnp.zeros((112, DEPTH), BF16)
     fl[pl.ds(800, 112), :] = jnp.zeros((112, DEPTH), BF16)
 
@@ -112,6 +104,15 @@
     def stage1(q, carry):
         c2, h = lax.rem(q, 2), q // 2
         base = pl.multiple_of(c2 * 400 + h * 256, 16)
+
+        def flat(b, carry):
+            at = pl.multiple_of(base + 16 * b, 16)
+            hi, lo = split(widen(cbuf[pl.ds(at, 16), :]))
+            fh[pl.ds(at, 16), :] = hi
+            fl[pl.ds(at, 16), :] = lo
+            return carry
+
+        lax.fori_loop(0, jnp.where(h == 0, 16, 9), flat, 0)
         acc = dot3(th[...], tl[...], fh[pl.ds(base, 256), :], fl[pl.ds(base, 256), :], NT)
         sent[2 * q] = acc[:, :128]
 
@@ -371,14 +372,13 @@
     lax.fori_loop(0, PAIRS, landed, 0)
 
 
-def arrange(o_ref, out_ref):
+def arrange(o_ref, out_ref, ready, sems):
+    lane = lax.broadcasted_iota(jnp.int32, (8, 128), 1)
+
     def plain(k, carry):
         for b in range(PAIRS // 8):
-            out_ref[k, pl.ds(8 * b, 8), :] = o_ref[pl.ds(8 * b * SLOT + k, 8, stride=SLOT), :][:, :COLS]
-        return carry
-
-    lax.fori_loop(0, SENT, plain, 0, unroll=6)
-    lane = lax.broadcasted_iota(jnp.int32, (8, 128), 1)
+            ready[k, pl.ds(8 * b, 8), :] = o_ref[pl.ds(8 * b * SLOT + k, 8, stride=SLOT), :][:, :COLS]
+        return carry
 
     def parts(q, carry):
         for b in range(PAIRS // 8):
@@ -387,10 +387,19 @@
                 part = o_ref[pl.ds(8 * b * SLOT + 8 * j + q, 8, stride=SLOT), :]
                 part = pltpu.roll(part, 28 + 25 * j, 1)
                 value = part if j == 0 else jnp.where(lane >= 25 * j, part, value)
-            out_ref[SENT + q, pl.ds(8 * b, 8), :] = value[:, :COLS]
-        return carry
-
-    lax.fori_loop(0, 8, parts, 0, unroll=2)
+            ready[SENT + q, pl.ds(8 * b, 8), :] = value[:, :COLS]
+        return carry
+
+    copies = []
+    for n, (start, rows) in enumerate(((SENT, 8), (0, 14), (14, 14), (28, 14))):
+        if start == SENT:
+            lax.fori_loop(0, 8, parts, 0, unroll=2)
+        else:
+            lax.fori_loop(start, start + rows, plain, 0, unroll=7)
+        copies.append(pltpu.make_async_copy(ready.at[pl.ds(start, rows)], out_ref.at[pl.ds(start, rows)], sems.at[n]))
+        copies[-1].start()
+    for copy in copies:
+        copy.wait()
 
 
 def on_device(integrals, coeffs):
@@ -430,7 +439,8 @@
         arrange,
         out_shape=jax.ShapeDtypeStruct((KROWS, PAIRS, COLS), F32),
         in_specs=[pl.BlockSpec(memory_space=pltpu.VMEM)],
-        out_specs=pl.BlockSpec(memory_space=pltpu.VMEM),
+        out_specs=pl.BlockSpec(memory_space=pl.ANY),
+        scratch_shapes=[pltpu.VMEM((KROWS, PAIRS, COLS), F32), dma((4,))],
         compiler_params=pltpu.CompilerParams(vmem_limit_bytes=16 * 2**20),
     )(blocks)
     return jnp.transpose(slab, (0, 2, 1))

time: 62.4 us -> 61.6 us (0.987)
  Pallas kernels: 62.3 us -> 61.5 us
where the time goes in v6:
time: 61.6 us; the launch traced here: 61.5 us
  Pallas kernels  61.5 us (100%)
    pallas_call x1, Pallas kernels, on_device(): pl.pallas_call(kernel, out_shape=jax.ShapeDtypeStruct(((PAIRS + 1) * SLOT...  59.6 us
    pallas_call x1, Pallas kernels, on_device(): pl.pallas_call(arrange, out_shape=jax.ShapeDtypeStruct((KROWS, PAIRS, COL...  1.84 us

profile of v6, /device:TPU:1, one launch (start us, length us, event | category | flops | bytes accessed | tf_op | source)
XLA Modules:
  0.0 61.5 jit_solution(11550835918029425538)
XLA Ops:
  0.0 59.6 %shard_map.28.o_ref = f32[3120,128]{1,0:T(8,128)S(1)} custom-call(f32[75,8,1200]{2,1,0:T(8,128)} %x_ref.1, f32[800,1200]{1,0:T(8,128)} %bitcast.2), custom_call_target="tpu_custom_call" | custom-call | tf_op jit(solution)/shard_map/pallas_call | solution.py:407
  59.6 1.8 %shard_map.29 = f32[50,64,100]{2,1,0:T(8,128)} custom-call(f32[3120,128]{1,0:T(8,128)S(1)} %shard_map.28.o_ref), custom_call_target="tpu_custom_call" | custom-call | tf_op jit(solution)/shard_map/pallas_call | solution.py:438

commit v7 on v6

--- a/solution.py
+++ b/solution.py
@@ -149,8 +149,8 @@
                 pltpu.make_async_copy(src, dst, l1).wait()
 
         def send(k, carry):
-            i = lax.rem(jnp.where(h == 0, k // 2, k) + g, 8)
-            e = jnp.where(h == 0, lax.rem(k, 2), 1 - k // 8)
+            i = lax.rem(k + g, 8)
+            e = 1 - k // 8
             j = 8 * c + i
             tile = 2 * h + e
 
@@ -329,7 +329,7 @@
 
     def left1(k, carry):
         q, kk = k // 16, lax.rem(k, 16)
-        j = 8 * c + lax.rem(jnp.where(q < 2, kk // 2, kk) + g, 8)
+        j = 8 * c + lax.rem(kk + g, 8)
         last = (q >= 2) & (kk < 8)
         moved = (j != g) | (lax.rem(q, 2) != c)
 

time: 61.6 us -> 61.5 us (level)
  no operation moved by 1% of the time
where the time goes in v7:
time: 61.5 us; the launch traced here: 61.4 us
  Pallas kernels  61.4 us (100%)
    pallas_call x1, Pallas kernels, on_device(): pl.pallas_call(kernel, out_shape=jax.ShapeDtypeStruct(((PAIRS + 1) * SLOT...  59.6 us
    pallas_call x1, Pallas kernels, on_device(): pl.pallas_call(arrange, out_shape=jax.ShapeDtypeStruct((KROWS, PAIRS, COL...  1.84 us

profile of v7, /device:TPU:1, one launch (start us, length us, event | category | flops | bytes accessed | tf_op | source)
XLA Modules:
  0.0 61.4 jit_solution(7175137433568259051)
XLA Ops:
  0.0 59.6 %shard_map.28.o_ref = f32[3120,128]{1,0:T(8,128)S(1)} custom-call(f32[75,8,1200]{2,1,0:T(8,128)} %x_ref.1, f32[800,1200]{1,0:T(8,128)} %bitcast.2), custom_call_target="tpu_custom_call" | custom-call | tf_op jit(solution)/shard_map/pallas_call | solution.py:407
  59.6 1.8 %shard_map.29 = f32[50,64,100]{2,1,0:T(8,128)} custom-call(f32[3120,128]{1,0:T(8,128)S(1)} %shard_map.28.o_ref), custom_call_target="tpu_custom_call" | custom-call | tf_op jit(solution)/shard_map/pallas_call | solution.py:438

commit v8 on v7

--- a/solution.py
+++ b/solution.py
@@ -213,7 +213,7 @@
                 al[pl.ds(at, 128), pl.ds(128 * e, 128)] = lo
             return carry
 
-        lax.fori_loop(0, DEPTH // 128, halves, 0)
+        lax.fori_loop(0, DEPTH // 128, halves, 0, unroll=5)
 
         def rows_of(half, carry):
             side = lax.rem(half + other, 2)

time: 61.5 us -> 61 us (level)
  no operation moved by 1% of the time
where the time goes in v8:
time: 61 us; the launch traced here: 60.9 us
  Pallas kernels  60.8 us (100%)
    pallas_call x1, Pallas kernels, on_device(): pl.pallas_call(kernel, out_shape=jax.ShapeDtypeStruct(((PAIRS + 1) * SLOT...  59 us
    pallas_call x1, Pallas kernels, on_device(): pl.pallas_call(arrange, out_shape=jax.ShapeDtypeStruct((KROWS, PAIRS, COL...  1.84 us

profile of v8, /device:TPU:1, one launch (start us, length us, event | category | flops | bytes accessed | tf_op | source)
XLA Modules:
  0.0 60.9 jit_solution(15911567848435259704)
XLA Ops:
  0.0 59.0 %shard_map.28.o_ref = f32[3120,128]{1,0:T(8,128)S(1)} custom-call(f32[75,8,1200]{2,1,0:T(8,128)} %x_ref.1, f32[800,1200]{1,0:T(8,128)} %bitcast.2), custom_call_target="tpu_custom_call" | custom-call | tf_op jit(solution)/shard_map/pallas_call | solution.py:407
  59.0 1.8 %shard_map.29 = f32[50,64,100]{2,1,0:T(8,128)} custom-call(f32[3120,128]{1,0:T(8,128)S(1)} %shard_map.28.o_ref), custom_call_target="tpu_custom_call" | custom-call | tf_op jit(solution)/shard_map/pallas_call | solution.py:438

commit v9 on v8

--- a/solution.py
+++ b/solution.py
@@ -213,7 +213,7 @@
                 al[pl.ds(at, 128), pl.ds(128 * e, 128)] = lo
             return carry
 
-        lax.fori_loop(0, DEPTH // 128, halves, 0, unroll=5)
+        lax.fori_loop(0, DEPTH // 128, halves, 0, unroll=10)
 
         def rows_of(half, carry):
             side = lax.rem(half + other, 2)

time: 61 us -> 60.9 us (level)
  no operation moved by 1% of the time
where the time goes in v9:
time: 60.9 us; the launch traced here: 60.8 us
  Pallas kernels  60.8 us (100%)
    pallas_call x1, Pallas kernels, on_device(): pl.pallas_call(kernel, out_shape=jax.ShapeDtypeStruct(((PAIRS + 1) * SLOT...  58.9 us
    pallas_call x1, Pallas kernels, on_device(): pl.pallas_call(arrange, out_shape=jax.ShapeDtypeStruct((KROWS, PAIRS, COL...  1.84 us

profile of v9, /device:TPU:1, one launch (start us, length us, event | category | flops | bytes accessed | tf_op | source)
XLA Modules:
  0.0 60.8 jit_solution(5467050583295685634)
XLA Ops:
  0.0 58.9 %shard_map.28.o_ref = f32[3120,128]{1,0:T(8,128)S(1)} custom-call(f32[75,8,1200]{2,1,0:T(8,128)} %x_ref.1, f32[800,1200]{1,0:T(8,128)} %bitcast.2), custom_call_target="tpu_custom_call" | custom-call | tf_op jit(solution)/shard_map/pallas_call | solution.py:407
  58.9 1.8 %shard_map.29 = f32[50,64,100]{2,1,0:T(8,128)} custom-call(f32[3120,128]{1,0:T(8,128)S(1)} %shard_map.28.o_ref), custom_call_target="tpu_custom_call" | custom-call | tf_op jit(solution)/shard_map/pallas_call | solution.py:438
